TPU v7x, 32 devices: a whole 2x2x4 slice. The times are simulated.
32 devices in a mesh: heads: 2 (over y), seq: 16 (over z, x, core).
Axes of the slice: x: 2, y: 2, z: 4, core: 2. Of those that a mesh axis runs over, the one named last changes fastest.
Arguments:
- queries: bfloat16 [2, 6144, 4096], P(None, 'seq', 'heads'), may hold values from -72 to 72, as said below
- key_rows: bfloat16 [2, 6144, 4096], P(None, 'seq', 'heads'), may hold values from -6.06 to 6.06, as said below
- value_rows: bfloat16 [2, 6144, 4096], P(None, 'seq', 'heads'), may hold values from -6 to 6
- step_rates: float32 [8, 2, 6144], P('heads', None, 'seq'), may hold values from 0.0001 to 0.001
- w_gate: float32 [8, 512, 512], P('heads', 'seq'), may hold values from -0.25 to 0.25
- w_up: float32 [8, 512, 512], P('heads', 'seq'), may hold values from -0.25 to 0.25
- w_down: float32 [8, 512, 512], P('heads', 'seq'), may hold values from -0.25 to 0.25
- out_gain: float32 [4096], P('heads'), may hold values from 0.5 to 1.5
Outputs:
- layer_out: bfloat16 [2, 6144, 4096], P(None, 'seq', 'heads')
- new_gate: float32 [8, 512, 512], P('heads', 'seq')
- new_up: float32 [8, 512, 512], P('heads', 'seq')
- new_down: float32 [8, 512, 512], P('heads', 'seq')
Inputs may be any that keep to these rules, and one draw needn't show every extreme that they name: `queries`: entries of order one with a few larger ones. `key_rows`: entries of order one.
All inputs are finite; a program needn't handle non-finite values.
Results may differ from a plain program's by a relative error of at most 0.0069.
The roundings to bfloat16 on the way count: a program that leaves them out, or rounds other values in their place, can miss the bound.
Values may be sent and summed in bfloat16 or wider, within the bound.
A program may use at most 192 MiB of HBM per device.

v0:
```python
import jax
import jax.numpy as jnp
from jax import lax
from jax.sharding import PartitionSpec as P

WINDOW = 768


NORM_EPS = 1e-05
MASKED = -1e30


def passed_along(value, axis, steps):
    count = lax.axis_size(axis)
    pairs = [(source, (source + steps) % count) for source in range(count)]
    return lax.ppermute(value, axis, pairs)


def fast_apply(inputs, copies):
    gate_copy, up_copy, down_copy = copies
    gate_pre = jnp.einsum("thd,hdf->thf", inputs, gate_copy, preferred_element_type=jnp.float32)
    up_pre = jnp.einsum("thd,hdf->thf", inputs, up_copy, preferred_element_type=jnp.float32)
    active = (jax.nn.silu(gate_pre) * up_pre).astype(jnp.bfloat16)
    return jnp.einsum("thf,hfd->thd", active, down_copy, preferred_element_type=jnp.float32)


def fast_grads(key_in, value_in, rate_in, copies):
    gate_copy, up_copy, down_copy = copies
    gate_pre = jnp.einsum("thd,hdf->thf", key_in, gate_copy, preferred_element_type=jnp.float32)
    up_pre = jnp.einsum("thd,hdf->thf", key_in, up_copy, preferred_element_type=jnp.float32)
    sigmoid_g = jax.nn.sigmoid(gate_pre)
    silu_g = gate_pre * sigmoid_g
    active = (silu_g * up_pre).astype(jnp.bfloat16)
    target = (-(rate_in[:, :, None] * value_in.astype(jnp.float32))).astype(jnp.bfloat16)
    grad_down = jnp.einsum("thf,thd->hfd", active, target, preferred_element_type=jnp.float32)
    back = jnp.einsum("thd,hfd->thf", target, down_copy, preferred_element_type=jnp.float32)
    d_gate = (back * up_pre * sigmoid_g * (1.0 + gate_pre * (1.0 - sigmoid_g))).astype(jnp.bfloat16)
    d_up = (back * silu_g).astype(jnp.bfloat16)
    grad_gate = jnp.einsum("thd,thf->hdf", key_in, d_gate, preferred_element_type=jnp.float32)
    grad_up = jnp.einsum("thd,thf->hdf", key_in, d_up, preferred_element_type=jnp.float32)
    return (grad_gate, grad_up, grad_down)


def carry_back(stacked):
    return jnp.concatenate([jnp.zeros_like(stacked[:, :1]), stacked[:, :-1]], axis=1)


def earlier_rows(key_rows, value_rows):
    tok_rows = key_rows.shape[1]
    hop_count = -(-WINDOW // tok_rows)
    seq_index = lax.axis_index("seq")
    own_pair = jnp.stack([key_rows, value_rows])
    gathered = []
    current = own_pair
    for hop_idx in range(hop_count):
        needed = min(tok_rows, WINDOW - hop_idx * tok_rows)
        sending = current
        arrived = passed_along(sending, "seq", 1)
        current = jnp.where(seq_index == 0, carry_back(arrived), arrived)
        gathered.insert(0, current)
    extended = jnp.concatenate(gathered + [own_pair], axis=2)
    return (extended[0], extended[1])


def window_attention(query_heads, keys_ext, values_ext, row_base):
    stretches, tok_rows, heads_dev, head_size = query_heads.shape
    key_span = keys_ext.shape[1]
    key_heads = keys_ext.reshape(stretches, key_span, heads_dev, head_size)
    value_heads = values_ext.reshape(stretches, key_span, heads_dev, head_size)
    scores = jnp.einsum(
        "cqhd,ckhd->chqk", query_heads, key_heads, preferred_element_type=jnp.float32
    ) * head_size ** (-0.5)
    query_pos = jnp.arange(tok_rows, dtype=jnp.int32)[:, None]
    key_pos = jnp.arange(key_span, dtype=jnp.int32)[None, :]
    inside = (key_pos > query_pos) & (key_pos <= query_pos + WINDOW)
    started = row_base[:, None, None, None] + key_pos[None, None] - WINDOW >= 0
    allowed = inside[None, None] & started
    scores = jnp.where(allowed, scores, MASKED)
    row_peak = jnp.max(scores, axis=-1, keepdims=True)
    weights = jnp.exp(scores - row_peak)
    soft_weights = (weights / jnp.sum(weights, axis=-1, keepdims=True)).astype(jnp.bfloat16)
    return jnp.einsum(
        "chqk,ckhd->cqhd", soft_weights, value_heads, preferred_element_type=jnp.float32
    )


def on_device(queries, key_rows, value_rows, step_rates, w_gate, w_up, w_down, out_gain):
    stretches, tok_rows, feat_width = queries.shape
    heads_dev = w_gate.shape[0]
    head_size = feat_width // heads_dev
    seq_index = lax.axis_index("seq")
    query_heads = queries.reshape(stretches, tok_rows, heads_dev, head_size)
    key_heads = key_rows.reshape(stretches, tok_rows, heads_dev, head_size)
    value_heads = value_rows.reshape(stretches, tok_rows, heads_dev, head_size)
    keys_ext, values_ext = earlier_rows(key_rows, value_rows)
    masters = (w_gate, w_up, w_down)
    first_rates = step_rates[:, 0, :].T
    full_masters = (
        lax.all_gather(masters[0], "seq", axis=1, tiled=True),
        lax.all_gather(masters[1], "seq", axis=1, tiled=True),
        lax.all_gather(masters[2], "seq", axis=1, tiled=True),
    )
    copies = tuple((member.astype(jnp.bfloat16) for member in full_masters))
    first_out = fast_apply(query_heads[0], copies)
    gradients = fast_grads(key_heads[0], value_heads[0], first_rates, copies)
    totals = lax.psum((gradients[0], gradients[1], gradients[2]), "seq")
    full_new = tuple((master - gradient for master, gradient in zip(full_masters, totals)))
    shard_rows = w_gate.shape[1]
    updated = tuple(
        (
            lax.dynamic_slice_in_dim(member, seq_index * shard_rows, shard_rows, 1)
            for member in full_new
        )
    )
    second_copies = tuple((member.astype(jnp.bfloat16) for member in full_new))
    second_out = fast_apply(query_heads[1], second_copies)
    fast_out = jnp.stack([first_out, second_out]).reshape(stretches, tok_rows, feat_width)
    row_power = jnp.sum(fast_out * fast_out, axis=-1, keepdims=True)
    total_power = lax.psum(row_power, "heads")
    normed = (
        fast_out
        * out_gain
        * lax.rsqrt(total_power / (feat_width * lax.axis_size("heads")) + NORM_EPS)
    )
    row_base = (
        jnp.arange(stretches, dtype=jnp.int32) * (tok_rows * lax.axis_size("seq"))
        + seq_index * tok_rows
    )
    attended = window_attention(query_heads, keys_ext, values_ext, row_base).reshape(
        stretches, tok_rows, feat_width
    )
    layer_out = (normed + attended).astype(jnp.bfloat16)
    return (layer_out, updated[0], updated[1], updated[2])


def solution(mesh):
    placed = (
        P(None, "seq", "heads"),
        P(None, "seq", "heads"),
        P(None, "seq", "heads"),
        P("heads", None, "seq"),
        P("heads", "seq", None),
        P("heads", "seq", None),
        P("heads", "seq", None),
        P("heads"),
    )
    return jax.shard_map(
        on_device,
        mesh=mesh,
        in_specs=placed,
        out_specs=(
            P(None, "seq", "heads"),
            P("heads", "seq", None),
            P("heads", "seq", None),
            P("heads", "seq", None),
        ),
        check_vma=False,
    )
```

profile of v0, /device:TPU:0, one launch (start us, length us, event | category | flops | bytes accessed | tf_op | source)
XLA Modules:
  0.0 521.5 jit_solution(1696891503598448490)
XLA Ops:
  7.2 1.8 copy.55
  9.1 1.8 copy.51
  11.0 4.6 copy.75
  15.6 3.4 copy.60
  19.1 5.3 %pad_maximum_fusion.1 = bf16[2,2,384,2048]{2,3,1,0:T(8,128)(2,1)} fusion(bf16[1,2,384,2048]{2,3,1,0:T(8,128)(2,1)} %bitcast.143, bf16[1,2,384,2048]{2,3,1,0:T(8,128)(2,1)S(1)} %bitcast.141), kind=kLoop, calls=%fused_computation.11 | loop fusion | flops 3145728 | bytes 12582912 | tf_op jit(solution)/shard_map/stack | solution.py:52
  25.0 1.3 slice.40
  26.2 3.5 slice_convert_fusion
  29.8 5.2 %reshape.111 = f32[384,4,512]{2,1,0:T(4,128)} reshape(f32[1,384,2048]{2,1,0:T(8,128)} %slice_convert_fusion) | data formatting | bytes 6291456 | tf_op jit(solution)/shard_map/convert_element_type | solution.py:34
  35.0 4.0 fusion.66
  39.0 2.6 copy.98
  41.7 2.6 copy.97
  44.6 100.4 %collective-permute-done = bf16[2,2,384,2048]{2,3,1,0:T(8,128)(2,1)} collective-permute-done((bf16[2,2,384,2048]{2,3,1,0:T(8,128)(2,1)}, bf16[2,2,384,2048]{2,3,1,0:T(8,128)(2,1)}, u32[]{:S(2)}, u32[]{:S(2)}) %collective-permute-start) | collective-permute-done | bytes 6291488 | tf_op jit(solution)/shard_map/ppermute | solution.py:16
  145.1 2.3 slice.41
  147.4 3.3 pad_select_fusion.1
  150.8 1.4 broadcast_and_fusion
  152.2 5.2 %copy.56 = f32[4,512,512]{1,2,0:T(8,128)} copy(f32[4,512,512]{2,0,1:T(4,128)} %all-gather.6.cloned.1.call-done) | data formatting | bytes 8388608 | tf_op jit(solution)/shard_map/all_gather | solution.py:100
  157.5 5.3 %copy.52 = f32[4,512,512]{1,2,0:T(8,128)} copy(f32[4,512,512]{2,0,1:T(4,128)} %all-gather.4.cloned.1.call-done) | data formatting | bytes 8388608 | tf_op jit(solution)/shard_map/all_gather | solution.py:99
  162.8 5.6 %fusion.54 = f32[4,512,384]{2,1,0:T(8,128)} fusion(bf16[384,4,512]{0,2,1:T(8,128)(2,1)} %bitcast.157, f32[4,512,512]{1,2,0:T(8,128)} %copy.52), kind=kOutput, calls=%fused_computation.75 | convolution fusion | flops 806354944 | bytes 8912896 | tf_op jit(solution)/shard_map/thd,hdf->thf/dot_general | solution.py:21
  168.4 26.5 %all-gather.8.cloned.1.call-done = f32[4,512,512]{2,1,0:T(8,128)} async-done(((f32[4,32,512]{2,1,0:T(8,128)}), f32[4,512,512]{2,1,0:T(8,128)}) %all-gather.8.cloned.1.call-update) | async-done | bytes 4194320 | tf_op jit(solution)/shard_map/all_gather | solution.py:101
  194.8 8.7 %convolution_bitcast_fusion.2 = f32[384,4,512]{2,0,1:T(8,128)} fusion(f32[4,512,384]{2,1,0:T(8,128)} %fusion.54, bf16[384,4,512]{0,2,1:T(8,128)(2,1)} %bitcast.158, f32[4,512,512]{2,1,0:T(8,128)} %all-gather.8.cloned.1.call-done, f32[4,512,512]{1,2,0:T(8,128)} %copy.56), kind=kOutput, calls=%fused_computation.60 | convolution fusion | flops 1617428480 | bytes 16252928 | tf_op jit(solution)/shard_map/thf,hfd->thd/dot_general | solution.py:24
  203.5 3.6 copy.59
  207.1 4.1 fusion.48
  211.5 1.3 fusion.52
  214.6 1.8 fusion.45
  216.4 3.2 convolution_bitcast_fusion
  219.6 3.5 fusion.36
  223.1 3.5 convolution_bitcast_fusion.1
  226.7 29.2 %collective-permute-done.1 = bf16[2,2,384,2048]{2,3,1,0:T(8,128)(2,1)} collective-permute-done((bf16[2,2,384,2048]{2,3,1,0:T(8,128)(2,1)}, bf16[2,2,384,2048]{2,3,1,0:T(8,128)(2,1)}, u32[]{:S(2)}, u32[]{:S(2)}) %collective-permute-start.1) | collective-permute-done | bytes 6291488 | tf_op jit(solution)/shard_map/ppermute | solution.py:16
  255.9 3.9 slice.42
  259.8 2.7 pad_select_fusion
  262.7 7.3 %maximum_maximum_fusion = bf16[2,2,1152,2048]{2,3,1,0:T(8,128)(2,1)S(1)} fusion(bf16[1,2,384,2048]{2,3,1,0:T(8,128)(2,1)S(1)} %bitcast.144, bf16[1,2,384,2048]{2,3,1,0:T(8,128)(2,1)S(1)} %bitcast.142, bf16[2,2,384,2048]{2,3,1,0:T(8,128)(2,1)} %pad_select_fusion.1, bf16[2,2,384,2048]{2,3,1,0:T(8,128)(2,1)S(1)} %pad_select_fusion), kind=kLoop, calls=%fused_computation.1 | loop fusion | flops 75497472 | bytes 37748736 | tf_op jit(solution)/shard_map/concatenate | solution.py:61
  270.0 7.5 %fusion.65 = (bf16[1,2,1152,2048]{2,3,1,0:T(8,128)(2,1)}, bf16[1,2,1152,2048]{2,3,1,0:T(8,128)(2,1)}) fusion(bf16[2,2,1152,2048]{2,3,1,0:T(8,128)(2,1)S(1)} %maximum_maximum_fusion), kind=kLoop, calls=%fused_computation.92 | loop fusion | bytes 37748736 | tf_op jit(solution)/shard_map/slice | solution.py:62
  277.5 14.3 %fusion.67 = (f32[2,4,384]{2,1,0:T(4,128)S(1)}, f32[2,4,384,1152]{2,3,1,0:T(8,128)}) fusion(pred[2,384,1152]{1,2,0:T(8,128)(4,1)} %broadcast_and_fusion, bf16[2,1152,4,512]{1,3,2,0:T(8,128)(2,1)} %bitcast.154, bf16[2,48,4,8,512]{4,3,2,1,0:T(8,128)(2,1)S(1)} %bitcast.159), kind=kOutput, calls=%fused_computation.94 | convolution fusion | flops 3638035456 | bytes 27635712 | tf_op jit(solution)/shard_map/sub | solution.py:80
  291.9 14.1 %fusion.4 = f32[2,4,512,384]{3,2,1,0:T(8,128)} fusion(bf16[2,1152,4,512]{1,3,2,0:T(8,128)(2,1)} %bitcast.153, f32[2,4,384,1152]{2,3,1,0:T(8,128)} %get-tuple-element.24, f32[2,4,384]{2,1,0:T(4,128)S(1)} %get-tuple-element.23), kind=kOutput, calls=%fused_computation.8 | convolution fusion | flops 3630956544 | bytes 29896704 | tf_op jit(solution)/shard_map/chqk,ckhd->cqhd/dot_general | solution.py:82
  306.0 162.8 %all-reduce.5.cloned.1.call-done = (f32[4,512,512]{2,1,0:T(8,128)}, f32[4,512,512]{1,2,0:T(8,128)}, f32[4,512,512]{1,2,0:T(8,128)}) async-done(((f32[4,512,512]{2,1,0:T(8,128)}, f32[4,512,512]{1,2,0:T(8,128)}, f32[4,512,512]{1,2,0:T(8,128)}), (f32[4,512,512]{2,1,0:T(8,128)}, f32[4,512,512]{1,2,0:T(8,128)}, f32[4,512,512]{1,2,0:T(8,128)})) %all-reduce.5.cloned.1.call-update) | async-done | bytes 12582928 | tf_op jit(solution)/shard_map/psum | solution.py:106
  468.7 4.7 sub.27
  473.4 1.2 copy-done.12
  474.7 1.0 sub.26
  476.1 2.9 fusion.29
  479.1 2.0 constant_dynamic-slice_fusion.1
  481.1 1.6 copy-done.5
  482.7 1.0 sub.24
  483.7 1.9 copy-done.10
  486.4 9.1 %fusion.33 = f32[4,512,384]{2,1,0:T(8,128)} fusion(f32[4,512,512]{2,1,0:T(8,128)} %copy-done.10, f32[4,512,384]{2,1,0:T(8,128)} %fusion.29, bf16[384,4,512]{0,2,1:T(8,128)(2,1)} %bitcast.155, f32[4,512,512]{1,2,0:T(8,128)} %copy-done.8), kind=kOutput, calls=%fused_computation.58 | convolution fusion | flops 1617428480 | bytes 16252928 | tf_op jit(solution)/shard_map/thf,hfd->thd/dot_general | solution.py:24
  495.4 2.4 multiply_reduce_fusion
  497.8 4.9 psum.31
  502.8 5.4 %fusion.6 = bf16[2,384,2048]{1,2,0:T(8,128)(2,1)} fusion(f32[2,4,512,384]{3,2,1,0:T(8,128)} %fusion.4, f32[1,384,2048]{1,2,0:T(8,128)} %bitcast.152, f32[1,384,2048]{1,2,0:T(8,128)S(1)} %bitcast.146, f32[2,384]{1,0:T(2,128)S(1)} %rsqrt_bitcast_fusion, f32[2048]{0:T(1024)S(1)} %copy-done.16), kind=kLoop, calls=%fused_computation.13 | loop fusion | flops 7864320 | bytes 15739904 | tf_op jit(solution)/shard_map/convert_element_type | solution.py:132
  508.1 4.8 copy.79
  (54 shorter events, 6.8 us)
Async XLA Ops:
  7.2 145.1 %all-gather.6.cloned.1.call-start = ((), (), s32[]{:S(2)}) async-start(), calls=%async_computation.1 | async-start | bytes 4456448 | tf_op jit(solution)/shard_map/all_gather | solution.py:100
  9.1 148.4 %all-gather.4.cloned.1.call-start = ((), (), s32[]{:S(2)}) async-start(), calls=%async_computation | async-start | bytes 4456448 | tf_op jit(solution)/shard_map/all_gather | solution.py:99
  11.0 183.9 %all-gather.8.cloned.1.call-start = ((), (), s32[]{:S(2)}) async-start(), calls=%async_computation.2 | async-start | bytes 4456448 | tf_op jit(solution)/shard_map/all_gather | solution.py:101
  24.4 120.7 %collective-permute-start = (bf16[2,2,384,2048]{2,3,1,0:T(8,128)(2,1)}, bf16[2,2,384,2048]{2,3,1,0:T(8,128)(2,1)}, u32[]{:S(2)}, u32[]{:S(2)}) collective-permute-start(bf16[2,2,384,2048]{2,3,1,0:T(8,128)(2,1)} %pad_maximum_fusion.1), channel_id=1, source_target_pairs={{0,1},{1,2},{2,3},{3,4},{4,5},{5,6},{6,7},{7,8},{8,9},{9,10},{10,1... | collective-permute-start | bytes 18874376 | tf_op jit(solution)/shard_map/ppermute | solution.py:16
  24.9 443.8 %all-reduce.5.cloned.1.call-start = ((), (), s32[]{:S(2)}) async-start(), calls=%async_computation.3 | async-start | bytes 25165824 | tf_op jit(solution)/shard_map/psum | solution.py:106
  29.8 5.2 %slice-start = ((f32[4,2,384]{2,1,0:T(2,128)}), f32[4,1,384]{2,1,0:T(1,128)S(1)}, s32[]{:S(2)}) async-start(f32[4,2,384]{2,1,0:T(2,128)} %param.11), calls=%async_computation.4 | async-start | bytes 12288 | tf_op jit(solution)/shard_map/slice | solution.py:97
  150.7 105.2 %collective-permute-start.1 = (bf16[2,2,384,2048]{2,3,1,0:T(8,128)(2,1)}, bf16[2,2,384,2048]{2,3,1,0:T(8,128)(2,1)}, u32[]{:S(2)}, u32[]{:S(2)}) collective-permute-start(bf16[2,2,384,2048]{2,3,1,0:T(8,128)(2,1)} %pad_select_fusion.1), channel_id=1, source_target_pairs={{0,1},{1,2},{2,3},{3,4},{4,5},{5,6},{6,7},{7,8},{8,9},{9,10},{10,1... | collective-permute-start | bytes 18874376 | tf_op jit(solution)/shard_map/ppermute | solution.py:16
  207.1 4.1 copy-start
  207.1 4.4 copy-start.6
  211.5 2.2 copy-start.4
  211.5 3.2 copy-start.7
  259.8 2.9 copy-start.2
  270.0 7.5 %copy-start.15 = (bf16[2,384,2048]{2,1,0:T(8,128)(2,1)S(1)}, bf16[2,384,2048]{2,1,0:T(8,128)(2,1)}, u32[]{:S(2)}) copy-start(bf16[2,384,2048]{2,1,0:T(8,128)(2,1)} %param.8) | copy-start | bytes 9437188
  468.7 4.7 copy-start.1
  468.7 5.9 %copy-start.12 = (f32[4,512,512]{1,2,0:T(8,128)S(1)}, f32[4,512,512]{1,2,0:T(8,128)}, u32[]{:S(2)}) copy-start(f32[4,512,512]{1,2,0:T(8,128)} %get-tuple-element.18) | copy-start | bytes 12582916
  474.7 1.4 copy-start.9
  475.7 3.5 copy-start.8
  476.1 5.0 copy-start.11
  479.1 3.5 copy-start.5
  483.7 2.0 copy-start.10
  486.4 9.1 %copy-start.3 = (f32[384,4,512]{0,2,1:T(8,128)S(1)}, f32[384,4,512]{0,2,1:T(8,128)}, u32[]{:S(2)}) copy-start(f32[384,4,512]{0,2,1:T(8,128)} %copy.59) | copy-start | bytes 9437188
  495.4 7.3 %copy-start.16 = (f32[2048]{0:T(1024)S(1)}, f32[2048]{0:T(1024)}, u32[]{:S(2)}) copy-start(f32[2048]{0:T(1024)} %param.15) | copy-start | bytes 24580
  508.1 4.8 copy-start.14
  508.1 5.8 %copy-start.13 = (f32[4,32,512]{1,2,0:T(8,128)S(1)}, f32[4,32,512]{1,2,0:T(8,128)}, u32[]{:S(2)}) copy-start(f32[4,32,512]{1,2,0:T(8,128)} %get-tuple-element.25) | copy-start | bytes 786436
Sparse Core Ops, SparseCore 0:
  10.7 59.8 all-gather.5
  73.3 60.7 all-gather.3
  136.3 58.4 all-gather.7
  226.8 241.8 all-reduce.4
where the time goes:
time: 523 us; the launch traced here: 521 us
  waiting for transfers between devices  319 us (61%)
  local copies, waits for them, and re-layouts  72.5 us (14%)
  matrix products  72 us (14%)
  other arithmetic  38.5 us (7%)
  between operations  13.9 us (3%)
    psum x1, waiting for transfers between devices, on_device(): totals = lax.psum((gradients[0], gradients[1], gradients[2]), 'seq')  163 us
    ppermute x2, waiting for transfers between devices, passed_along(): return lax.ppermute(value, axis, pairs)  130 us
    unnamed x44, local copies, waits for them, and re-layouts  31.4 us
    all_gather x1, waiting for transfers between devices, on_device(): lax.all_gather(masters[2], 'seq', axis=1, tiled=True)  26.5 us
    dot_general x2, matrix products, fast_apply(): jnp.einsum('thf,hfd->thd', active, down_copy, preferred_element_type=jnp....  17.7 us
    sub x1, matrix products, window_attention(): weights = jnp.exp(scores - row_peak)  14.3 us
    dot_general x1, matrix products, window_attention(): jnp.einsum('chqk,ckhd->cqhd', soft_weights, value_heads, preferred_elemen...  14.1 us
  transfers between devices with their start and end apart: 6, of which 4 were waited for; matrix products, arithmetic and copies ran while one was open for 26% of the time, Pallas kernels for 0%

commit v1 on v0

v1 whole, which is shorter than its diff:
```python
import functools

import jax
import jax.numpy as jnp
from jax import lax
from jax.experimental import pallas as pl
from jax.experimental.pallas import tpu as pltpu
from jax.sharding import PartitionSpec as P

WINDOW = 768
NORM_EPS = 1e-05
MASKED = -1e30
VMEM = 56 * 1024 * 1024
F32 = jnp.float32
BF16 = jnp.bfloat16


def dot(a, b, contract=((1,), (0,))):
    return lax.dot_general(a, b, (contract, ((), ())), preferred_element_type=F32)


def passed_along(value, axis, steps):
    count = lax.axis_size(axis)
    pairs = [(source, (source + steps) % count) for source in range(count)]
    return lax.ppermute(value, axis, pairs)


def groups():
    count = lax.axis_size("seq")
    near = 2 if count % 2 == 0 else 1
    far = count // near
    inside = [[i * near + j for j in range(near)] for i in range(far)]
    across = [[i * near + j for i in range(far)] for j in range(near)]
    return inside, across


def gather_two_level(value):
    inside, across = groups()
    return lax.all_gather(value, "seq", axis=0)[None]


def scatter_two_level(value):
    inside, across = groups()
    return lax.psum_scatter(value[0], "seq", scatter_dimension=0)


def params():
    return pltpu.CompilerParams(vmem_limit_bytes=VMEM)


def weights_of(w_ref, which):
    near, far = w_ref.shape[:2]
    return jnp.concatenate(
        [w_ref[i % near, i // near, 0, which] for i in range(near * far)], axis=0
    )


def grads_kernel(w_ref, k_ref, v_ref, r_ref, out_ref):
    head = pl.program_id(0)
    near, far, _, _, rows, cols = w_ref.shape
    k = k_ref[0]
    lane = lax.broadcasted_iota(jnp.int32, r_ref.shape, 1)
    rate = jnp.sum(jnp.where(lane == head, r_ref[...], 0.0), axis=1, keepdims=True)
    g = dot(k, weights_of(w_ref, 0))
    u = dot(k, weights_of(w_ref, 1))
    target = (-(rate * v_ref[0].astype(F32))).astype(BF16)
    back = dot(target, weights_of(w_ref, 2), ((1,), (1,)))
    sig = jax.nn.sigmoid(g)
    silu = g * sig
    active = (silu * u).astype(BF16)
    d_gate = (back * u * sig * (1.0 + g * (1.0 - sig))).astype(BF16)
    d_up = (back * silu).astype(BF16)
    first = ((0,), (0,))
    pairs = ((active, target), (k, d_gate), (k, d_up))
    for which, (left, right) in zip((2, 0, 1), pairs):
        full = dot(left, right, first).astype(BF16)
        for i in range(near * far):
            out_ref[i % near, i // near, 0, which] = full[i * rows : (i + 1) * rows]


def fast_grads(copies, key_rows, value_rows, rates):
    near, far, heads, _, rows, cols = copies.shape
    tok = key_rows.shape[1]
    size = near * far * rows
    w_spec = pl.BlockSpec((near, far, 1, 3, rows, cols), lambda h: (0, 0, h, 0, 0, 0))
    t_spec = pl.BlockSpec((1, tok, size), lambda h: (0, 0, h))
    return pl.pallas_call(
        grads_kernel,
        grid=(heads,),
        in_specs=[w_spec, t_spec, t_spec, pl.BlockSpec(rates.shape, lambda h: (0, 0))],
        out_specs=w_spec,
        out_shape=jax.ShapeDtypeStruct(copies.shape, BF16),
        compiler_params=params(),
        cost_estimate=pl.CostEstimate(
            flops=heads * tok * size * cols * 12,
            bytes_accessed=copies.size * 4 + tok * heads * size * 4,
            transcendentals=heads * tok * cols,
        ),
        name="fast_grads",
    )(copies, key_rows, value_rows, rates)


def apply_kernel(w_ref, q_ref, out_ref, power_ref):
    head = pl.program_id(0)
    q = q_ref[0]
    g = dot(q, weights_of(w_ref, 0))
    u = dot(q, weights_of(w_ref, 1))
    active = (g * jax.nn.sigmoid(g) * u).astype(BF16)
    out = dot(active, weights_of(w_ref, 2))
    out_ref[...] = out
    power = jnp.sum(out * out, axis=1, keepdims=True)

    @pl.when(head == 0)
    def _():
        power_ref[...] = power

    @pl.when(head > 0)
    def _():
        power_ref[...] += power


def fast_apply(copies, queries, stretch):
    near, far, heads, _, rows, cols = copies.shape
    tok = queries.shape[1]
    size = near * far * rows
    return pl.pallas_call(
        apply_kernel,
        grid=(heads,),
        in_specs=[
            pl.BlockSpec((near, far, 1, 3, rows, cols), lambda h: (0, 0, h, 0, 0, 0)),
            pl.BlockSpec((1, tok, size), lambda h: (stretch, 0, h)),
        ],
        out_specs=[
            pl.BlockSpec((tok, size), lambda h: (0, h)),
            pl.BlockSpec((tok, 1), lambda h: (0, 0)),
        ],
        out_shape=[
            jax.ShapeDtypeStruct((tok, heads * size), F32),
            jax.ShapeDtypeStruct((tok, 1), F32),
        ],
        compiler_params=params(),
        cost_estimate=pl.CostEstimate(
            flops=heads * tok * size * cols * 6,
            bytes_accessed=copies.size * 2 + tok * heads * size * 6,
            transcendentals=heads * tok * cols,
        ),
        name="fast_apply",
    )(copies, queries)


def attend_kernel(hops, stretch, seq_ref, q_ref, *refs):
    keys = refs[: hops + 1]
    values = refs[hops + 1 : 2 * hops + 2]
    out_ref = refs[-1]
    q = q_ref[0]
    tok, size = q.shape
    row = lax.broadcasted_iota(jnp.int32, (tok, tok), 0)
    col = lax.broadcasted_iota(jnp.int32, (tok, tok), 1)
    scores = []
    for hop in range(hops + 1):
        s = dot(q, keys[hop][0], ((1,), (1,))) * size ** (-0.5)
        place = col - hop * tok
        if hop == 0:
            s = jnp.where(place <= row, s, MASKED)
        if (hop + 1) * tok > WINDOW:
            s = jnp.where(place > row - WINDOW, s, MASKED)
        if hop > 0 and stretch == 0:
            s = jnp.where(seq_ref[0] >= hop, s, MASKED)
        scores.append(s)
    peak = functools.reduce(jnp.maximum, [jnp.max(s, axis=1, keepdims=True) for s in scores])
    weights = [jnp.exp(s - peak) for s in scores]
    total = functools.reduce(jnp.add, [jnp.sum(w, axis=1, keepdims=True) for w in weights])
    scale = 1.0 / total
    out = None
    for hop in range(hops + 1):
        part = dot((weights[hop] * scale).astype(BF16), values[hop][0])
        out = part if out is None else out + part
    if len(refs) == 2 * hops + 3:
        out_ref[...] = out
    else:
        fast_ref, gain_ref, inv_ref = refs[2 * hops + 2 : 2 * hops + 5]
        out_ref[0] = (fast_ref[...] * gain_ref[...] * inv_ref[...] + out).astype(BF16)


def attend(seq, stretch, queries, keys, values, heads, normed=None):
    stretches, tok, feat = queries.shape
    size = feat // heads
    hops = len(keys) - 1

    def rows_of(hop):
        def index(h, seq_ref):
            back = jnp.where(seq_ref[0] < hop, 1, 0)
            return (jnp.maximum(stretch - back, 0), 0, h)

        return pl.BlockSpec((1, tok, size), index)

    token_specs = [rows_of(hop) for hop in range(hops + 1)]
    in_specs = [pl.BlockSpec((1, tok, size), lambda h, s: (stretch, 0, h))] + token_specs * 2
    operands = [seq, queries, *keys, *values]
    if normed is None:
        out_specs = pl.BlockSpec((tok, size), lambda h, s: (0, h))
        out_shape = jax.ShapeDtypeStruct((tok, feat), F32)
    else:
        operands += list(normed)
        in_specs += [
            pl.BlockSpec((tok, size), lambda h, s: (0, h)),
            pl.BlockSpec((1, size), lambda h, s: (0, h)),
            pl.BlockSpec((tok, 1), lambda h, s: (0, 0)),
        ]
        out_specs = pl.BlockSpec((1, tok, size), lambda h, s: (stretch, 0, h))
        out_shape = jax.ShapeDtypeStruct((stretches, tok, feat), BF16)
    return pl.pallas_call(
        functools.partial(attend_kernel, hops, stretch),
        grid_spec=pltpu.PrefetchScalarGridSpec(
            num_scalar_prefetch=1,
            grid=(heads,),
            in_specs=in_specs,
            out_specs=out_specs,
        ),
        out_shape=out_shape,
        compiler_params=params(),
        cost_estimate=pl.CostEstimate(
            flops=feat * tok * tok * (hops + 1) * 4 * 2,
            bytes_accessed=feat * tok * (2 * (2 * hops + 3) + 4),
            transcendentals=heads * tok * tok * (hops + 1),
        ),
        name="attend",
    )(*operands)


def final_kernel(stretch, base_ref, fast_ref, gain_ref, inv_ref, att_ref, out_ref):
    out_ref[0] = (fast_ref[...] * gain_ref[...] * inv_ref[...] + att_ref[...]).astype(BF16)


def finish(base, stretch, fast, gain, inv, att, parts):
    _, tok, feat = base.shape
    size = feat // parts
    tall = pl.BlockSpec((tok, size), lambda h: (0, h))
    return pl.pallas_call(
        functools.partial(final_kernel, stretch),
        grid=(parts,),
        in_specs=[
            pl.BlockSpec(memory_space=pl.ANY),
            tall,
            pl.BlockSpec((1, size), lambda h: (0, h)),
            pl.BlockSpec((tok, 1), lambda h: (0, 0)),
            tall,
        ],
        out_specs=pl.BlockSpec((1, tok, size), lambda h: (stretch, 0, h)),
        out_shape=jax.ShapeDtypeStruct(base.shape, base.dtype),
        input_output_aliases={0: 0},
        compiler_params=params(),
        name="finish",
    )(base, fast, gain, inv, att)


def on_device(queries, key_rows, value_rows, step_rates, w_gate, w_up, w_down, out_gain):
    stretches, tok, feat = queries.shape
    heads = w_gate.shape[0]
    seq = lax.axis_index("seq").astype(jnp.int32).reshape(1)
    hops = -(-WINDOW // tok)
    features = feat * lax.axis_size("heads")
    gain = out_gain.reshape(1, feat)

    def inverse_norm(power):
        total = lax.psum(power.reshape(tok), "heads")
        return lax.rsqrt(total / features + NORM_EPS).reshape(tok, 1)

    masters = jnp.stack([w_gate, w_up, w_down], axis=1)
    copies = gather_two_level(masters.astype(BF16))
    keys, values = [key_rows], [value_rows]
    keys.append(passed_along(key_rows, "seq", 1))
    values.append(passed_along(value_rows, "seq", 1))
    copies, keys[1], values[1] = lax.optimization_barrier((copies, keys[1], values[1]))
    for _ in range(1, hops):
        keys.append(passed_along(keys[-1], "seq", 1))
        values.append(passed_along(values[-1], "seq", 1))

    gradients = fast_grads(copies, key_rows, value_rows, step_rates[:, 0, :].T)
    total = scatter_two_level(gradients)
    fast_0, power_0 = fast_apply(copies, queries, 0)
    inv_0 = inverse_norm(power_0)
    total, keys, values, fast_0, inv_0 = lax.optimization_barrier(
        (total, keys, values, fast_0, inv_0)
    )
    updated = masters - total.astype(F32)
    second = gather_two_level(updated.astype(BF16))
    layer_0 = attend(seq, 0, queries, keys, values, heads, (fast_0, gain, inv_0))
    attended_1 = attend(seq, 1, queries, keys, values, heads)
    second, layer_0, attended_1 = lax.optimization_barrier((second, layer_0, attended_1))
    fast_1, power_1 = fast_apply(second, queries, 1)
    layer_out = finish(layer_0, 1, fast_1, gain, inverse_norm(power_1), attended_1, heads)
    return (layer_out, updated[:, 0], updated[:, 1], updated[:, 2])


def solution(mesh):
    rows = P(None, "seq", "heads")
    weights = P("heads", "seq", None)
    return jax.shard_map(
        on_device,
        mesh=mesh,
        in_specs=(rows, rows, rows, P("heads", None, "seq"), weights, weights, weights, P("heads")),
        out_specs=(rows, weights, weights, weights),
        check_vma=False,
    )
```

time: 523 us -> 333 us (0.64)
  waiting for transfers between devices: 319 us -> 243 us
  matrix products: 72 us -> 0 us
  local copies, waits for them, and re-layouts: 72.5 us -> 4.06 us
  Pallas kernels: 0 us -> 50.9 us
  other arithmetic: 38.5 us -> 7.05 us
    psum x1 -> x0, waiting for transfers between devices: 163 us -> none  [on_device(): totals = lax.psum((gradients[0], gradients[1], gradients[2]), 'seq')]
    ppermute x2 -> x4, waiting for transfers between devices: 130 us -> 206 us  [passed_along(): return lax.ppermute(value, axis, pairs)]
    dot_general x11 -> x0, matrix products: 57.7 us -> none  [the longest x2 17.7 us: fast_apply(): jnp.einsum('thf,hfd->thd', active, down_copy, preferred_element_type=jnp....]
    pallas_call x0 -> x6, Pallas kernels: none -> 50.9 us  [the longest x2 20.8 us: attend(): pl.pallas_call(functools.partial(attend_kernel, hops, stretch), grid_spec...]
    unnamed x44 -> x5, local copies, waits for them, and re-layouts: 31.4 us -> 0.84 us
    slice x7 -> x1, local copies, waits for them, and re-layouts: 19 us -> 0.71 us  [on_device(): gradients = fast_grads(copies, key_rows, value_rows, step_rates[:, 0, :].T)]
    sub x1 -> x0, matrix products: 14.3 us -> none  [window_attention(): weights = jnp.exp(scores - row_peak)]
    all_gather x3 -> x2, waiting for transfers between devices: 26.5 us -> 37.3 us  [gather_two_level(): return lax.all_gather(value, 'seq', axis=0)[None]]
  transfers between devices with their start and end apart: 6 -> 7, of which waited for: 4 -> 5; matrix products, arithmetic and copies ran while one was open for 26% -> 1% of each run, Pallas kernels for 0% -> 8%
where the time goes in v1:
time: 333 us; the launch traced here: 332 us
  waiting for transfers between devices  243 us (73%)
  Pallas kernels  50.9 us (15%)
  between operations  13.8 us (4%)
  blocking collectives  9.88 us (3%)
  other arithmetic  7.05 us (2%)
  local copies, waits for them, and re-layouts  4.06 us (1%)
  starting transfers between devices  3.34 us (1%)
    ppermute x4, waiting for transfers between devices, passed_along(): return lax.ppermute(value, axis, pairs)  206 us
    all_gather x2, waiting for transfers between devices, gather_two_level(): return lax.all_gather(value, 'seq', axis=0)[None]  37.3 us
    pallas_call x2, Pallas kernels, attend(): pl.pallas_call(functools.partial(attend_kernel, hops, stretch), grid_spec...  20.8 us
    pallas_call x2, Pallas kernels, fast_apply(): pl.pallas_call(apply_kernel, grid=(heads,), in_specs=[pl.BlockSpec((near,...  14.4 us
    pallas_call x1, Pallas kernels, fast_grads(): pl.pallas_call(grads_kernel, grid=(heads,), in_specs=[w_spec, t_spec, t_s...  10.7 us
    psum x2, blocking collectives, inverse_norm(): total = lax.psum(power.reshape(tok), 'heads')  9.88 us
  transfers between devices with their start and end apart: 7, of which 5 were waited for; matrix products, arithmetic and copies ran while one was open for 1% of the time, Pallas kernels for 8%

profile of v1, /device:TPU:0, one launch (start us, length us, event | category | flops | bytes accessed | tf_op | source)
XLA Modules:
  0.0 332.0 jit_solution(6158656070985305382)
XLA Ops:
  7.2 0.0 all-gather.4.cloned.1.call-start
  7.2 1.0 convert_bitcast_fusion.2
  8.2 1.1 convert_bitcast_fusion
  9.3 0.8 pad_maximum_fusion
  10.0 0.0 all-gather.4.cloned.1.call-update
  10.1 0.0 reduce-scatter.2.cloned.1.call-start
  10.1 0.5 collective-permute-start
  10.6 2.6 collective-permute-start.1
  13.2 0.7 slice.12
  13.9 0.8 copy.20
  14.8 65.6 %collective-permute-done.refs_1_ = bf16[2,384,2048]{2,1,0:T(8,128)(2,1)S(1)} collective-permute-done((bf16[2,384,2048]{2,1,0:T(8,128)(2,1)}, bf16[2,384,2048]{2,1,0:T(8,128)(2,1)S(1)}, u32[]{:S(2)}, u32[]{:S(2)}) %collective-permute-start) | collective-permute-done | bytes 3145760 | tf_op jit(solution)/shard_map/ppermute | solution.py:25
  80.4 0.0 copy-start
  80.4 42.2 %collective-permute-done.1.refs_4_ = bf16[2,384,2048]{2,1,0:T(8,128)(2,1)} collective-permute-done((bf16[2,384,2048]{2,1,0:T(8,128)(2,1)}, bf16[2,384,2048]{2,1,0:T(8,128)(2,1)}, u32[]{:S(2)}, u32[]{:S(2)}) %collective-permute-start.1) | collective-permute-done | bytes 3145760 | tf_op jit(solution)/shard_map/ppermute | solution.py:25
  122.5 0.0 all-gather.4.cloned.1.call-done
  122.5 10.7 %fast_grads.1 = bf16[1,16,4,3,32,512]{5,4,3,2,1,0:T(8,128)(2,1)} custom-call(bf16[1,16,4,3,32,512]{5,4,3,2,1,0:T(8,128)(2,1)} %bitcast.24, bf16[2,384,2048]{2,1,0:T(8,128)(2,1)} %refs_0_.1, bf16[2,384,2048]{2,1,0:T(8,128)(2,1)} %refs_3_.1, f32[384,4]{1,0:T(8,128)} %bitcast.31), custom_call_target="tpu_custom_call" | custom-call | flops 4831838208 | bytes 15728640 | tf_op jit(solution)/shard_map/fast_grads/pallas_call | solution.py:87
  133.3 0.0 reduce-scatter.2.cloned.1.call-update
  133.3 0.0 copy-start.1
  133.3 0.0 all-gather.6.cloned.1.call-start
  133.3 0.0 copy-done
  133.4 0.1 collective-permute-start.2
  133.4 0.1 collective-permute-start.3
  133.5 7.2 %fast_apply.2 = (f32[384,2048]{1,0:T(8,128)}, f32[384,1]{1,0:T(8,128)}) custom-call(bf16[1,16,4,3,32,512]{5,4,3,2,1,0:T(8,128)(2,1)} %bitcast.25, bf16[2,384,2048]{2,1,0:T(8,128)(2,1)} %q_ref.7), custom_call_target="tpu_custom_call" | custom-call | flops 2415919104 | bytes 11010048 | tf_op jit(solution)/shard_map/fast_apply/pallas_call | solution.py:126
  140.7 1.1 reduce
  141.8 4.9 %psum.14 = f32[384]{0:T(512)S(1)} all-reduce(f32[384]{0:T(512)S(1)} %reduce), channel_id=1, replica_groups=mesh['heads'=2,'seq'=16] {'heads'}, use_global_device_ids=true, to_apply=%region_1.0 | all-reduce | flops 384 | bytes 3072 | tf_op jit(solution)/shard_map/psum | solution.py:266
  146.7 31.1 %collective-permute-done.2.refs_2_ = bf16[2,384,2048]{2,1,0:T(8,128)(2,1)} collective-permute-done((bf16[2,384,2048]{2,1,0:T(8,128)(2,1)S(1)}, bf16[2,384,2048]{2,1,0:T(8,128)(2,1)}, u32[]{:S(2)}, u32[]{:S(2)}) %collective-permute-start.2) | collective-permute-done | bytes 3145760 | tf_op jit(solution)/shard_map/ppermute | solution.py:25
  177.8 66.9 %collective-permute-done.3.refs_5_ = bf16[2,384,2048]{2,1,0:T(8,128)(2,1)} collective-permute-done((bf16[2,384,2048]{2,1,0:T(8,128)(2,1)}, bf16[2,384,2048]{2,1,0:T(8,128)(2,1)}, u32[]{:S(2)}, u32[]{:S(2)}) %collective-permute-start.3) | collective-permute-done | bytes 3145760 | tf_op jit(solution)/shard_map/ppermute | solution.py:25
  244.6 0.0 reduce-scatter.2.cloned.1.call-done
  244.6 0.0 copy-done.1
  244.6 2.1 fusion
  246.7 0.0 all-gather.6.cloned.1.call-update
  246.7 0.8 copy.18.refs_8_
  247.5 0.9 slice_bitcast_fusion
  248.4 10.3 %attend.3.att_ref = f32[384,2048]{1,0:T(8,128)} custom-call(s32[1]{0:T(128)} %bitcast.12.seq_ref, bf16[2,384,2048]{2,1,0:T(8,128)(2,1)} %q_ref.7, bf16[2,384,2048]{2,1,0:T(8,128)(2,1)} %refs_0_.1, bf16[2,384,2048]{2,1,0:T(8,128)(2,1)} %copy-done, bf16[2,384,2048]{2,1,0:T(8,128)(2,1)} %collective-permute-done.2.refs_2_, bf16[2,384,2048]{2,1,0:T(8,128)(2,1)} %refs_3_.1, ...), custom_call_target="tpu_custom_call" | custom-call | flops 7247757312 | bytes 14155776 | tf_op jit(solution)/shard_map/attend/pallas_call | solution.py:212
  258.8 10.5 %attend.2.base_ref = bf16[2,384,2048]{2,1,0:T(8,128)(2,1)} custom-call(s32[1]{0:T(128)} %bitcast.12.seq_ref, bf16[2,384,2048]{2,1,0:T(8,128)(2,1)} %q_ref.7, bf16[2,384,2048]{2,1,0:T(8,128)(2,1)} %refs_0_.1, bf16[2,384,2048]{2,1,0:T(8,128)(2,1)} %copy-done, bf16[2,384,2048]{2,1,0:T(8,128)(2,1)} %collective-permute-done.2.refs_2_, ...), custom_call_target="tpu_custom_call" | custom-call | flops 7247757312 | bytes 14155776 | tf_op jit(solution)/shard_map/attend/pallas_call | solution.py:212
  269.2 37.3 %all-gather.6.cloned.1.call-done = bf16[64,3,32,512]{3,2,1,0:T(8,128)(2,1)} async-done(((bf16[4,3,32,512]{3,2,1,0:T(8,128)(2,1)}), bf16[64,3,32,512]{3,2,1,0:T(8,128)(2,1)}) %all-gather.6.cloned.1.call-update) | async-done | bytes 6291472 | tf_op jit(solution)/shard_map/all_gather | solution.py:39
  306.5 7.2 %fast_apply.3 = (f32[384,2048]{1,0:T(8,128)}, f32[384,1]{1,0:T(8,128)}) custom-call(bf16[1,16,4,3,32,512]{5,4,3,2,1,0:T(8,128)(2,1)} %bitcast.27, bf16[2,384,2048]{2,1,0:T(8,128)(2,1)} %q_ref.7), custom_call_target="tpu_custom_call" | custom-call | flops 2415919104 | bytes 11010048 | tf_op jit(solution)/shard_map/fast_apply/pallas_call | solution.py:126
  313.7 1.1 reduce.1
  314.7 4.9 %psum.15 = f32[384]{0:T(512)S(1)} all-reduce(f32[384]{0:T(512)S(1)} %reduce.1), channel_id=1, replica_groups=mesh['heads'=2,'seq'=16] {'heads'}, use_global_device_ids=true, to_apply=%region_2.0 | all-reduce | flops 384 | bytes 3072 | tf_op jit(solution)/shard_map/psum | solution.py:266
  319.7 0.8 reshape.82.inv_ref
  320.5 5.0 %finish.1 = bf16[2,384,2048]{2,1,0:T(8,128)(2,1)} custom-call(bf16[2,384,2048]{2,1,0:T(8,128)(2,1)} %attend.2.base_ref, f32[384,2048]{1,0:T(8,128)} %get-tuple-element.39.fast_ref, f32[1,2048]{1,0:T(1,128)} %bitcast.34, f32[384,1]{1,0:T(8,128)} %reshape.82.inv_ref, f32[384,2048]{1,0:T(8,128)} %attend.3.att_ref), custom_call_target="tpu_custom_call", output_to_operand_aliasing={{}: (0, {})} | custom-call | tf_op jit(solution)/shard_map/finish/pallas_call | solution.py:239
  (3 shorter events, 0.0 us)
Async XLA Ops:
  7.2 115.4 %all-gather.4.cloned.1.call-start = ((), (), s32[]{:S(2)}) async-start(), calls=%async_computation.1 | async-start | bytes 6684672 | tf_op jit(solution)/shard_map/all_gather | solution.py:39
  10.1 234.6 %reduce-scatter.2.cloned.1.call-start = ((), (), s32[]{:S(2)}) async-start(), calls=%async_computation.2 | async-start | bytes 6684672 | tf_op jit(solution)/shard_map/reduce_scatter | solution.py:44
  10.1 70.2 %collective-permute-start = (bf16[2,384,2048]{2,1,0:T(8,128)(2,1)}, bf16[2,384,2048]{2,1,0:T(8,128)(2,1)S(1)}, u32[]{:S(2)}, u32[]{:S(2)}) collective-permute-start(bf16[2,384,2048]{2,1,0:T(8,128)(2,1)} %refs_0_.1), channel_id=1, source_target_pairs={{0,1},{1,2},{2,3},{3,4},{4,5},{5,6},{6,7},{7,8},{8,9},{9,10},{10,1... | collective-permute-start | bytes 9437192 | tf_op jit(solution)/shard_map/ppermute | solution.py:25
  10.6 111.9 %collective-permute-start.1 = (bf16[2,384,2048]{2,1,0:T(8,128)(2,1)}, bf16[2,384,2048]{2,1,0:T(8,128)(2,1)}, u32[]{:S(2)}, u32[]{:S(2)}) collective-permute-start(bf16[2,384,2048]{2,1,0:T(8,128)(2,1)} %refs_3_.1), channel_id=1, source_target_pairs={{0,1},{1,2},{2,3},{3,4},{4,5},{5,6},{6,7},{7,8},{8,9},{9,10},{10,1... | collective-permute-start | bytes 9437192 | tf_op jit(solution)/shard_map/ppermute | solution.py:25
  80.4 53.0 %copy-start = (bf16[2,384,2048]{2,1,0:T(8,128)(2,1)}, bf16[2,384,2048]{2,1,0:T(8,128)(2,1)S(1)}, u32[]{:S(2)}) copy-start(bf16[2,384,2048]{2,1,0:T(8,128)(2,1)S(1)} %collective-permute-done.refs_1_) | copy-start | bytes 9437188
  133.3 111.3 %copy-start.1 = (f32[4,32,512]{2,1,0:T(8,128)S(1)}, f32[4,32,512]{2,1,0:T(8,128)}, u32[]{:S(2)}) copy-start(f32[4,32,512]{2,1,0:T(8,128)} %param.14) | copy-start | bytes 786436
  133.3 173.2 %all-gather.6.cloned.1.call-start = ((), (), s32[]{:S(2)}) async-start(), calls=%async_computation.3 | async-start | bytes 6684672 | tf_op jit(solution)/shard_map/all_gather | solution.py:39
  133.4 44.4 %collective-permute-start.2 = (bf16[2,384,2048]{2,1,0:T(8,128)(2,1)S(1)}, bf16[2,384,2048]{2,1,0:T(8,128)(2,1)}, u32[]{:S(2)}, u32[]{:S(2)}) collective-permute-start(bf16[2,384,2048]{2,1,0:T(8,128)(2,1)S(1)} %collective-permute-done.refs_1_), channel_id=1, source_target_pairs={{0,1},{1,2},{2,3},{3,4},{4,5},{5,6},{6,7},{7,8},{8,9},{9,10},{10,1... | collective-permute-start | bytes 9437192 | tf_op jit(solution)/shard_map/ppermute | solution.py:25
  133.4 111.2 %collective-permute-start.3 = (bf16[2,384,2048]{2,1,0:T(8,128)(2,1)}, bf16[2,384,2048]{2,1,0:T(8,128)(2,1)}, u32[]{:S(2)}, u32[]{:S(2)}) collective-permute-start(bf16[2,384,2048]{2,1,0:T(8,128)(2,1)} %collective-permute-done.1.refs_4_), channel_id=1, source_target_pairs={{0,1},{1,2},{2,3},{3,4},{4,5},{5,6},{6,7},{7,8},{8,9},{9,10},{10,1... | collective-permute-start | bytes 9437192 | tf_op jit(solution)/shard_map/ppermute | solution.py:25
Sparse Core Ops, SparseCore 0:
  10.9 78.2 all-gather.3
  133.4 104.8 reduce-scatter.1
  246.8 59.5 all-gather.5
